TPU v7x, 32 devices: a whole 2x2x4 slice. The times are simulated.
32 devices in a mesh: row: 8 (over z, core), col: 4 (over y, x).
Axes of the slice: x: 2, y: 2, z: 4, core: 2. Of those that a mesh axis runs over, the one named last changes fastest.
Arguments:
- loads: float32 [48, 1024, 4096], P(None, 'row', 'col'), may hold values from -6 to 6
- below_first: float32 [47, 1024, 1024], P(None, 'row', 'col'), may hold values from -0.1875 to 0.1875
- below_second: float32 [46, 1024, 1024], P(None, 'row', 'col'), may hold values from -0.1875 to 0.1875
- inverses: float32 [2, 1024, 1024], P(None, None, 'row'), may hold values from -1 to 2, as said below
Outputs:
- solved: float32 [2, 1024, 4096], P(None, None, 'col')
- remaining: float32 [46, 1024, 4096], P(None, 'row', 'col')
Inputs may be any that keep to these rules, and one draw needn't show every extreme that they name: `inverses`: each of the two matrices is lower triangular, with a diagonal from 0.5 to 2.
All inputs are finite; a program needn't handle non-finite values.
Results may differ from a plain program's by a relative error of at most 0.000084.
Values sent between devices are 32-bit elements; how exact they have to be, the bound alone decides.
A program may use at most 256 MiB of HBM per device.

v0:
```python
import jax
import jax.numpy as jnp
from jax import lax
from jax.sharding import PartitionSpec as P


def solve_block(inverse_part, block_rows):
    partial_value = jnp.dot(inverse_part, block_rows, precision=lax.Precision.HIGHEST)
    return lax.psum(partial_value, "row")


def strip_product(shard_piece, solution):
    columns = shard_piece.shape[2]
    flattened = shard_piece.reshape(-1, columns)
    return jnp.dot(flattened, solution, precision=lax.Precision.HIGHEST)


def local(loads, below_first, below_second, inverses):
    cycles, rows_dev, rhs_dev = loads.shape
    first_block = solve_block(inverses[0], loads[0])
    updated = loads[1:].reshape(-1, rhs_dev) - strip_product(
        lax.all_gather(below_first, "col", axis=2, tiled=True), first_block
    )
    updated = updated.reshape(cycles - 1, rows_dev, rhs_dev)
    second_block = solve_block(inverses[1], updated[0])
    remaining = updated[1:].reshape(-1, rhs_dev) - strip_product(
        lax.all_gather(below_second, "col", axis=2, tiled=True), second_block
    )
    solved = jnp.stack([first_block, second_block])
    return (solved, remaining.reshape(cycles - 2, rows_dev, rhs_dev))


def solution(mesh):
    in_specs = (
        P(None, "row", "col"),
        P(None, "row", "col"),
        P(None, "row", "col"),
        P(None, None, "row"),
    )
    out_specs = (P(None, None, "col"), P(None, "row", "col"))
    return jax.shard_map(local, mesh=mesh, in_specs=in_specs, out_specs=out_specs, check_vma=False)
```

profile of v0, /device:TPU:0, one launch (start us, length us, event | category | flops | bytes accessed | tf_op | source)
XLA Modules:
  0.0 741.3 jit_solution(17923245185394723700)
XLA Ops:
  8.0 0.0 all-reduce.3.cloned.1.call-start
  8.0 6.6 fusion.2
  14.7 0.0 all-reduce.3.cloned.1.call-update
  14.7 0.0 all-gather.3.cloned.1.call-start
  14.8 0.5 all-gather.3.cloned.1.call-update
  15.3 0.0 all-gather.5.cloned.1.call-start
  15.3 0.5 all-gather.5.cloned.1.call-update
  15.9 0.0 all-reduce.5.cloned.1.call-start
  15.9 19.4 %slice.22 = f32[47,128,1024]{2,1,0:T(8,128)} slice(f32[48,128,1024]{2,1,0:T(8,128)} %param.4), slice={[1:48], [0:128], [0:1024]} | slice | bytes 49283072 | tf_op jit(solution)/shard_map/slice | solution.py:21
  35.3 24.9 %copy.9 = f32[6016,1024]{0,1:T(8,128)} copy(f32[6016,1024]{1,0:T(8,128)} %bitcast.25) | data formatting | bytes 49283072 | tf_op jit(solution)/shard_map/reshape | solution.py:21
  60.3 53.8 %all-reduce.3.cloned.1.call-done = f32[1024,1024]{1,0:T(8,128)} async-done(((f32[1024,1024]{1,0:T(8,128)}), f32[1024,1024]{1,0:T(8,128)}) %all-reduce.3.cloned.1.call-update) | async-done | bytes 4194320 | tf_op jit(solution)/shard_map/psum | solution.py:9
  114.1 128.8 %all-gather.3.cloned.1.call-done = f32[47,128,1024]{2,1,0:T(8,128)} async-done(((f32[47,128,256]{2,1,0:T(8,128)}), f32[47,128,1024]{2,1,0:T(8,128)}) %all-gather.3.cloned.1.call-update) | async-done | bytes 24641552 | tf_op jit(solution)/shard_map/all_gather | solution.py:22
  242.8 0.0 copy-start
  242.8 178.1 %bitcast_subtract_fusion = f32[6016,1024]{0,1:T(8,128)} fusion(f32[6016,1024]{0,1:T(8,128)} %copy.9, f32[1024,1024]{1,0:T(8,128)} %all-reduce.3.cloned.1.call-done, f32[6016,1024]{1,0:T(8,128)} %bitcast.29), kind=kOutput, calls=%fused_computation | convolution fusion | flops 75704958976 | bytes 78118912 | tf_op jit(solution)/shard_map/dot_general | solution.py:15
  421.0 0.0 copy-done
  421.0 6.0 convolution_bitcast_fusion
  427.0 0.0 all-reduce.5.cloned.1.call-update
  427.0 36.3 %all-gather.5.cloned.1.call-done = f32[46,128,1024]{2,1,0:T(8,128)} async-done(((f32[46,128,256]{2,1,0:T(8,128)}), f32[46,128,1024]{2,1,0:T(8,128)}) %all-gather.5.cloned.1.call-update) | async-done | bytes 24117264 | tf_op jit(solution)/shard_map/all_gather | solution.py:27
  463.4 60.8 %all-reduce.5.cloned.1.call-done = f32[1024,1024]{1,0:T(8,128)} async-done(((f32[1024,1024]{1,0:T(8,128)}), f32[1024,1024]{1,0:T(8,128)}) %all-reduce.5.cloned.1.call-update) | async-done | bytes 4194320 | tf_op jit(solution)/shard_map/psum | solution.py:9
  524.1 176.9 %slice_subtract_fusion = f32[5888,1024]{0,1:T(8,128)} fusion(f32[6016,1024]{0,1:T(8,128)} %bitcast_subtract_fusion, f32[1024,1024]{1,0:T(8,128)} %all-reduce.5.cloned.1.call-done, f32[5888,1024]{1,0:T(8,128)} %bitcast.30), kind=kOutput, calls=%fused_computation.1 | convolution fusion | flops 74094215168 | bytes 76546048 | tf_op jit(solution)/shard_map/dot_general | solution.py:15
  701.0 24.1 %copy.11 = f32[5888,1024]{1,0:T(8,128)} copy(f32[5888,1024]{0,1:T(8,128)} %slice_subtract_fusion) | data formatting | bytes 48234496 | tf_op jit(solution)/shard_map/sub | solution.py:26
  725.1 8.5 %pad_maximum_fusion = f32[2,1024,1024]{2,1,0:T(8,128)} fusion(f32[1,1024,1024]{2,1,0:T(8,128)} %bitcast.28, f32[1,1024,1024]{2,1,0:T(8,128)} %bitcast.27), kind=kLoop, calls=%fused_computation.2 | loop fusion | flops 2097152 | bytes 16777216 | tf_op jit(solution)/shard_map/stack | solution.py:29
Async XLA Ops:
  8.0 106.1 %all-reduce.3.cloned.1.call-start = ((), (), s32[]{:S(2)}) async-start(), calls=%async_computation | async-start | bytes 8388608 | tf_op jit(solution)/shard_map/psum | solution.py:9
  14.7 228.1 %all-gather.3.cloned.1.call-start = ((), (), s32[]{:S(2)}) async-start(), calls=%async_computation.1 | async-start | bytes 30801920 | tf_op jit(solution)/shard_map/all_gather | solution.py:22
  15.3 448.1 %all-gather.5.cloned.1.call-start = ((), (), s32[]{:S(2)}) async-start(), calls=%async_computation.3 | async-start | bytes 30146560 | tf_op jit(solution)/shard_map/all_gather | solution.py:27
  15.9 508.3 %all-reduce.5.cloned.1.call-start = ((), (), s32[]{:S(2)}) async-start(), calls=%async_computation.2 | async-start | bytes 8388608 | tf_op jit(solution)/shard_map/psum | solution.py:9
  242.8 178.1 %copy-start = (f32[2,1024,128]{2,1,0:T(8,128)S(1)}, f32[2,1024,128]{2,1,0:T(8,128)}, u32[]{:S(2)}) copy-start(f32[2,1024,128]{2,1,0:T(8,128)} %param.7) | copy-start | bytes 3145732
Sparse Core Ops, SparseCore 0:
  14.8 99.2 all-reduce.2
  427.1 96.9 all-reduce.4
Sparse Core Ops, SparseCore 1:
  17.0 225.8 all-gather.2
  244.6 218.7 all-gather.4
where the time goes:
time: 746 us; the launch traced here: 741 us
  matrix products  368 us (49%)
  waiting for transfers between devices  281 us (38%)
  local copies, waits for them, and re-layouts  68.4 us (9%)
  between operations  15.7 us (2%)
  other arithmetic  8.53 us (1%)
    dot_general x2, matrix products, strip_product(): return jnp.dot(flattened, solution, precision=lax.Precision.HIGHEST)  355 us
    all_gather x1, waiting for transfers between devices, local(): lax.all_gather(below_first, 'col', axis=2, tiled=True)  129 us
    psum x2, waiting for transfers between devices, solve_block(): return lax.psum(partial_value, 'row')  115 us
    all_gather x1, waiting for transfers between devices, local(): lax.all_gather(below_second, 'col', axis=2, tiled=True)  36.3 us
    reshape x1, local copies, waits for them, and re-layouts, local(): loads[1:].reshape(-1, rhs_dev)  24.9 us
    sub x1, local copies, waits for them, and re-layouts, local(): updated[1:].reshape(-1, rhs_dev)  24.1 us
    slice x1, local copies, waits for them, and re-layouts, local(): loads[1:].reshape(-1, rhs_dev)  19.4 us
  transfers between devices with their start and end apart: 4, of which 4 were waited for; matrix products, arithmetic and copies ran while one was open for 31% of the time, Pallas kernels for 0%

commit v1 on v0

--- a/solution.py
+++ b/solution.py
@@ -2,6 +2,19 @@
 import jax.numpy as jnp
 from jax import lax
 from jax.sharding import PartitionSpec as P
+
+
+def ring_gather(array, axis, dim):
+    ways = lax.axis_size(axis)
+    up = [(d, (d + 1) % ways) for d in range(ways)]
+    down = [(d, (d - 1) % ways) for d in range(ways)]
+    earlier, later = ([array], [array])
+    for _ in range(ways // 2):
+        earlier.append(lax.ppermute(earlier[-1], axis, up))
+    for _ in range((ways - 1) // 2):
+        later.append(lax.ppermute(later[-1], axis, down))
+    line = jnp.concatenate([*earlier[::-1], *later[1:]], axis=dim)
+    return jnp.roll(line, (lax.axis_index(axis) - ways // 2) * array.shape[dim], axis=dim)
 
 
 def solve_block(inverse_part, block_rows):
@@ -19,7 +32,7 @@
     cycles, rows_dev, rhs_dev = loads.shape
     first_block = solve_block(inverses[0], loads[0])
     updated = loads[1:].reshape(-1, rhs_dev) - strip_product(
-        lax.all_gather(below_first, "col", axis=2, tiled=True), first_block
+        ring_gather(below_first, "col", 2), first_block
     )
     updated = updated.reshape(cycles - 1, rows_dev, rhs_dev)
     second_block = solve_block(inverses[1], updated[0])

time: 746 us -> 867 us (1.16)
  waiting for transfers between devices: 281 us -> 570 us
  matrix products: 368 us -> 180 us
  local copies, waits for them, and re-layouts: 68.4 us -> 86.4 us
    ppermute x0 -> x3, waiting for transfers between devices: none -> 358 us  [the longest x2 244 us: ring_gather(): earlier.append(lax.ppermute(earlier[-1], axis, up))]
    dot_general x2, matrix products: 355 us -> 169 us  [strip_product(): return jnp.dot(flattened, solution, precision=lax.Precision.HIGHEST)]
    all_gather x1 -> x0, waiting for transfers between devices: 129 us -> none  [local(): lax.all_gather(below_first, 'col', axis=2, tiled=True)]
    all_gather x1, waiting for transfers between devices: 36.3 us -> 116 us  [local(): lax.all_gather(below_second, 'col', axis=2, tiled=True)]
    unnamed x2 -> x15, local copies, waits for them, and re-layouts: 0.01 us -> 45.1 us
    reshape x1 -> x0, local copies, waits for them, and re-layouts: 24.9 us -> none  [local(): loads[1:].reshape(-1, rhs_dev)]
    sub x1 -> x0, local copies, waits for them, and re-layouts: 24.1 us -> none  [local(): updated[1:].reshape(-1, rhs_dev)]
    psum x2, waiting for transfers between devices: 115 us -> 95.5 us  [solve_block(): return lax.psum(partial_value, 'row')]
  transfers between devices with their start and end apart: 4 -> 6, of which waited for: 4 -> 5; matrix products, arithmetic and copies ran while one was open for 31% -> 11% of each run, Pallas kernels for 0% -> 0%
where the time goes in v1:
time: 867 us
  waiting for transfers between devices  570 us (66%)
  matrix products  180 us (21%)
  local copies, waits for them, and re-layouts  86.4 us (10%)
  between operations  15.5 us (2%)
  other arithmetic  8.86 us (1%)
    ppermute x2, waiting for transfers between devices, ring_gather(): earlier.append(lax.ppermute(earlier[-1], axis, up))  244 us
    dot_general x2, matrix products, strip_product(): return jnp.dot(flattened, solution, precision=lax.Precision.HIGHEST)  169 us
    all_gather x1, waiting for transfers between devices, local(): lax.all_gather(below_second, 'col', axis=2, tiled=True)  116 us
    ppermute x1, waiting for transfers between devices, ring_gather(): later.append(lax.ppermute(later[-1], axis, down))  115 us
    psum x2, waiting for transfers between devices, solve_block(): return lax.psum(partial_value, 'row')  95.5 us
    unnamed x15, local copies, waits for them, and re-layouts  45.1 us
    slice x1, local copies, waits for them, and re-layouts, local(): loads[1:].reshape(-1, rhs_dev)  17.6 us
    dynamic_slice x1, local copies, waits for them, and re-layouts, ring_gather(): jnp.roll(line, (lax.axis_index(axis) - ways // 2) * array.shape[dim], axi...  17.6 us
  transfers between devices with their start and end apart: 6, of which 5 were waited for; matrix products, arithmetic and copies ran while one was open for 11% of the time, Pallas kernels for 0%

profile of v1, /device:TPU:0, one launch (start us, length us, event | category | flops | bytes accessed | tf_op | source)
XLA Modules:
  0.0 866.9 jit_solution(7101745965652469120)
XLA Ops:
  8.0 0.0 all-reduce.3.cloned.1.call-start
  8.0 3.0 collective-permute-start
  11.0 134.0 %collective-permute-done = f32[47,128,256]{2,1,0:T(8,128)} collective-permute-done((f32[47,128,256]{2,1,0:T(8,128)}, f32[47,128,256]{2,1,0:T(8,128)}, u32[]{:S(2)}, u32[]{:S(2)}) %collective-permute-start) | collective-permute-done | bytes 6160416 | tf_op jit(solution)/shard_map/ppermute | solution.py:13
  145.0 0.8 collective-permute-start.1
  145.8 2.1 collective-permute-start.2
  147.9 6.6 fusion.2
  154.6 0.0 all-reduce.3.cloned.1.call-update
  154.6 0.0 all-reduce.5.cloned.1.call-start
  154.7 17.6 %slice.22 = f32[47,128,1024]{2,1,0:T(8,128)} slice(f32[48,128,1024]{2,1,0:T(8,128)} %param.4), slice={[1:48], [0:128], [0:1024]} | slice | bytes 49283072 | tf_op jit(solution)/shard_map/slice | solution.py:34
  172.3 0.0 slice-start
  172.3 0.0 slice-start.1
  172.3 109.6 %collective-permute-done.1 = f32[47,128,256]{2,1,0:T(8,128)} collective-permute-done((f32[47,128,256]{2,1,0:T(8,128)}, f32[47,128,256]{2,1,0:T(8,128)}, u32[]{:S(2)}, u32[]{:S(2)}) %collective-permute-start.1) | collective-permute-done | bytes 6160416 | tf_op jit(solution)/shard_map/ppermute | solution.py:13
  281.9 6.1 constant_dynamic-update-slice_fusion.7
  288.0 6.2 constant_dynamic-update-slice_fusion.6
  294.2 0.0 slice-done
  294.2 0.0 slice-done.1
  294.2 3.1 constant_dynamic-update-slice_fusion.5
  297.3 114.7 %collective-permute-done.2 = f32[47,128,256]{2,1,0:T(8,128)} collective-permute-done((f32[47,128,256]{2,1,0:T(8,128)}, f32[47,128,256]{2,1,0:T(8,128)}, u32[]{:S(2)}, u32[]{:S(2)}) %collective-permute-start.2) | collective-permute-done | bytes 6160416 | tf_op jit(solution)/shard_map/ppermute | solution.py:15
  412.1 6.1 constant_dynamic-update-slice_fusion.4
  418.2 6.1 constant_dynamic-update-slice_fusion.3
  424.3 6.1 constant_dynamic-update-slice_fusion.2
  430.4 3.2 constant_dynamic-update-slice_fusion.1
  433.6 6.1 constant_dynamic-update-slice_fusion
  439.7 17.6 %constant_dynamic-slice_fusion = f32[47,128,1024]{2,1,0:T(8,128)} fusion(f32[47,128,2048]{2,1,0:T(8,128)} %constant_dynamic-update-slice_fusion, s32[]{:T(128)S(6)} %select_n.14), kind=kLoop, calls=%fused_computation.20 | loop fusion | bytes 49283076 | tf_op jit(solution)/shard_map/jit(_roll_dynamic)/dynamic_slice | solution.py:17
  457.3 0.0 all-reduce.3.cloned.1.call-done
  457.3 0.0 copy-start
  457.3 84.0 %bitcast_subtract_fusion = f32[6016,1024]{1,0:T(8,128)S(1)} fusion(f32[47,128,1024]{2,1,0:T(8,128)} %slice.22, f32[6016,1024]{1,0:T(8,128)} %bitcast.24, f32[1024,1024]{1,0:T(8,128)} %all-reduce.3.cloned.1.call-done), kind=kOutput, calls=%fused_computation | convolution fusion | flops 75704958976 | bytes 78118912 | tf_op jit(solution)/shard_map/dot_general | solution.py:28
  541.3 0.0 copy-start.1
  541.3 8.1 copy-done.1
  549.5 0.0 copy-done
  549.5 5.0 convolution_bitcast_fusion
  554.4 0.0 all-reduce.5.cloned.1.call-update
  554.4 0.0 all-gather.2.cloned.1.call-start
  554.5 0.5 all-gather.2.cloned.1.call-update
  555.0 95.5 %all-reduce.5.cloned.1.call-done = f32[1024,1024]{1,0:T(8,128)} async-done(((f32[1024,1024]{1,0:T(8,128)}), f32[1024,1024]{1,0:T(8,128)}) %all-reduce.5.cloned.1.call-update) | async-done | bytes 4194320 | tf_op jit(solution)/shard_map/psum | solution.py:22
  650.5 8.9 %pad_maximum_fusion = f32[2,1024,1024]{2,1,0:T(8,128)} fusion(f32[1,1024,1024]{2,1,0:T(8,128)} %bitcast.28, f32[1,1024,1024]{2,1,0:T(8,128)} %bitcast.27), kind=kLoop, calls=%fused_computation.2 | loop fusion | flops 2097152 | bytes 16777216 | tf_op jit(solution)/shard_map/stack | solution.py:42
  659.4 115.6 %all-gather.2.cloned.1.call-done = f32[46,128,1024]{2,1,0:T(8,128)} async-done(((f32[46,128,256]{2,1,0:T(8,128)}), f32[46,128,1024]{2,1,0:T(8,128)}) %all-gather.2.cloned.1.call-update) | async-done | bytes 24117264 | tf_op jit(solution)/shard_map/all_gather | solution.py:40
  775.0 84.5 %slice_subtract_fusion = f32[5888,1024]{1,0:T(8,128)} fusion(f32[6016,1024]{1,0:T(8,128)} %copy-done.1, f32[1024,1024]{1,0:T(8,128)} %all-reduce.5.cloned.1.call-done, f32[5888,1024]{1,0:T(8,128)} %bitcast.29), kind=kOutput, calls=%fused_computation.1 | convolution fusion | flops 74094215168 | bytes 76546048 | tf_op jit(solution)/shard_map/dot_general | solution.py:28
  (1 shorter events, 0.0 us)
Async XLA Ops:
  8.0 449.3 %all-reduce.3.cloned.1.call-start = ((), (), s32[]{:S(2)}) async-start(), calls=%async_computation | async-start | bytes 8388608 | tf_op jit(solution)/shard_map/psum | solution.py:22
  8.0 137.0 %collective-permute-start = (f32[47,128,256]{2,1,0:T(8,128)}, f32[47,128,256]{2,1,0:T(8,128)}, u32[]{:S(2)}, u32[]{:S(2)}) collective-permute-start(f32[47,128,256]{2,1,0:T(8,128)} %param.5), channel_id=1, source_target_pairs={{0,1},{1,2},{2,3},{3,0},{4,5},{5,6},{6,7},{7,4},{8,9},{9,10},{10,1... | collective-permute-start | bytes 18481160 | tf_op jit(solution)/shard_map/ppermute | solution.py:13
  145.0 136.9 %collective-permute-start.1 = (f32[47,128,256]{2,1,0:T(8,128)}, f32[47,128,256]{2,1,0:T(8,128)}, u32[]{:S(2)}, u32[]{:S(2)}) collective-permute-start(f32[47,128,256]{2,1,0:T(8,128)} %collective-permute-done), channel_id=1, source_target_pairs={{0,1},{1,2},{2,3},{3,0},{4,5},{5,6},{6,7},{7,4},{8,9},{9,10},{10,1... | collective-permute-start | bytes 18481160 | tf_op jit(solution)/shard_map/ppermute | solution.py:13
  145.8 266.3 %collective-permute-start.2 = (f32[47,128,256]{2,1,0:T(8,128)}, f32[47,128,256]{2,1,0:T(8,128)}, u32[]{:S(2)}, u32[]{:S(2)}) collective-permute-start(f32[47,128,256]{2,1,0:T(8,128)} %param.5), channel_id=1, source_target_pairs={{0,3},{1,0},{2,1},{3,2},{4,7},{5,4},{6,5},{7,6},{8,11},{9,8},{10,9... | collective-permute-start | bytes 18481160 | tf_op jit(solution)/shard_map/ppermute | solution.py:15
  154.6 495.9 %all-reduce.5.cloned.1.call-start = ((), (), s32[]{:S(2)}) async-start(), calls=%async_computation.1 | async-start | bytes 8388608 | tf_op jit(solution)/shard_map/psum | solution.py:22
  172.3 121.9 %slice-start = ((s8[6160384]{0:T(1024)(128)(4,1)}), s8[1966080]{0:T(1024)(128)(4,1)S(1)}, s32[]{:S(2)}) async-start(s8[6160384]{0:T(1024)(128)(4,1)} %bitcast.25), calls=%async_computation.3 | async-start | bytes 3932160
  172.3 121.9 %slice-start.1 = ((s8[6160384]{0:T(1024)(128)(4,1)}), s8[4194304]{0:T(1024)(128)(4,1)S(1)}, s32[]{:S(2)}) async-start(s8[6160384]{0:T(1024)(128)(4,1)} %bitcast.25), calls=%async_computation.4 | async-start | bytes 8388608
  457.3 92.2 %copy-start = (f32[2,1024,128]{2,1,0:T(8,128)S(1)}, f32[2,1024,128]{2,1,0:T(8,128)}, u32[]{:S(2)}) copy-start(f32[2,1024,128]{2,1,0:T(8,128)} %param.7) | copy-start | bytes 3145732
  541.3 8.1 copy-start.1
  554.4 220.5 %all-gather.2.cloned.1.call-start = ((), (), s32[]{:S(2)}) async-start(), calls=%async_computation.2 | async-start | bytes 30146560 | tf_op jit(solution)/shard_map/all_gather | solution.py:40
Sparse Core Ops, SparseCore 0:
  154.7 97.0 all-reduce.2
  554.5 95.9 all-reduce.4
Sparse Core Ops, SparseCore 1:
  556.8 218.1 all-gather.1

commit v2 on v0

--- a/solution.py
+++ b/solution.py
@@ -6,7 +6,7 @@
 
 def solve_block(inverse_part, block_rows):
     partial_value = jnp.dot(inverse_part, block_rows, precision=lax.Precision.HIGHEST)
-    return lax.psum(partial_value, "row")
+    return jnp.sum(lax.all_gather(partial_value, "row"), axis=0)
 
 
 def strip_product(shard_piece, solution):

time: 746 us -> 1340 us (1.80)
  waiting for transfers between devices: 281 us -> 907 us
  matrix products: 368 us -> 261 us
  local copies, waits for them, and re-layouts: 68.4 us -> 109 us
  other arithmetic: 8.53 us -> 39.1 us
    all_gather x0 -> x2, waiting for transfers between devices: none -> 534 us  [solve_block(): return jnp.sum(lax.all_gather(partial_value, 'row'), axis=0)]
    all_gather x1, waiting for transfers between devices: 36.3 us -> 166 us  [local(): lax.all_gather(below_second, 'col', axis=2, tiled=True)]
    psum x2 -> x0, waiting for transfers between devices: 115 us -> none  [solve_block(): return lax.psum(partial_value, 'row')]
    dot_general x2, matrix products: 355 us -> 249 us  [strip_product(): return jnp.dot(flattened, solution, precision=lax.Precision.HIGHEST)]
    all_gather x1, waiting for transfers between devices: 129 us -> 205 us  [local(): lax.all_gather(below_first, 'col', axis=2, tiled=True)]
    unnamed x2 -> x3, local copies, waits for them, and re-layouts: 0.01 us -> 34.9 us
    reduce_sum x0 -> x2, other arithmetic: none -> 30.6 us  [solve_block(): return jnp.sum(lax.all_gather(partial_value, 'row'), axis=0)]
  transfers between devices with their start and end apart: 4 -> 4, of which waited for: 4 -> 4; matrix products, arithmetic and copies ran while one was open for 31% -> 9% of each run, Pallas kernels for 0% -> 0%
where the time goes in v2:
time: 1340 us; the launch traced here: 1330 us
  waiting for transfers between devices  907 us (68%)
  matrix products  261 us (19%)
  local copies, waits for them, and re-layouts  109 us (8%)
  other arithmetic  39.1 us (3%)
  between operations  14 us (1%)
    all_gather x2, waiting for transfers between devices, solve_block(): return jnp.sum(lax.all_gather(partial_value, 'row'), axis=0)  534 us
    dot_general x2, matrix products, strip_product(): return jnp.dot(flattened, solution, precision=lax.Precision.HIGHEST)  249 us
    all_gather x1, waiting for transfers between devices, local(): lax.all_gather(below_first, 'col', axis=2, tiled=True)  205 us
    all_gather x1, waiting for transfers between devices, local(): lax.all_gather(below_second, 'col', axis=2, tiled=True)  166 us
    unnamed x3, local copies, waits for them, and re-layouts  34.9 us
    reduce_sum x2, other arithmetic, solve_block(): return jnp.sum(lax.all_gather(partial_value, 'row'), axis=0)  30.6 us
  transfers between devices with their start and end apart: 4, of which 4 were waited for; matrix products, arithmetic and copies ran while one was open for 9% of the time, Pallas kernels for 0%

profile of v2, /device:TPU:0, one launch (start us, length us, event | category | flops | bytes accessed | tf_op | source)
XLA Modules:
  0.0 1330.6 jit_solution(4640615532271035752)
XLA Ops:
  7.2 0.0 all-gather.11.cloned.1.call-start
  7.2 6.6 fusion.2
  13.8 0.0 all-gather.11.cloned.1.call-update
  13.9 0.0 all-gather.7.cloned.1.call-start
  13.9 0.7 all-gather.7.cloned.1.call-update
  14.6 0.0 all-gather.13.cloned.1.call-start
  14.7 19.3 %slice.22 = f32[47,128,1024]{2,1,0:T(8,128)} slice(f32[48,128,1024]{2,1,0:T(8,128)} %param.4), slice={[1:48], [0:128], [0:1024]} | slice | bytes 49283072 | tf_op jit(solution)/shard_map/slice | solution.py:21
  33.9 25.2 %copy.13 = f32[6016,1024]{0,1:T(8,128)} copy(f32[6016,1024]{1,0:T(8,128)} %bitcast.31) | data formatting | bytes 49283072 | tf_op jit(solution)/shard_map/reshape | solution.py:21
  59.1 246.2 %all-gather.11.cloned.1.call-done = f32[8192,1024]{1,0:T(8,128)} async-done(((f32[1024,1024]{1,0:T(8,128)}), f32[8192,1024]{1,0:T(8,128)}) %all-gather.11.cloned.1.call-update) | async-done | bytes 33554448 | tf_op jit(solution)/shard_map/all_gather | solution.py:9
  305.4 18.0 %reduce_sum.18 = f32[1024,1024]{1,0:T(8,128)} reduce(f32[8,1024,1024]{2,1,0:T(8,128)} %bitcast.32, f32[]{:T(128)} %constant.0.clone.1), dimensions={0}, to_apply=%region_0.0 | reduce | flops 7340032 | bytes 37748740 | tf_op jit(solution)/shard_map/reduce_sum | solution.py:9
  323.3 205.4 %all-gather.7.cloned.1.call-done = f32[47,128,1024]{2,1,0:T(8,128)} async-done(((f32[47,128,256]{2,1,0:T(8,128)}), f32[47,128,1024]{2,1,0:T(8,128)}) %all-gather.7.cloned.1.call-update) | async-done | bytes 24641552 | tf_op jit(solution)/shard_map/all_gather | solution.py:22
  528.7 0.0 copy-start
  528.7 163.4 %bitcast_subtract_fusion = f32[6016,1024]{0,1:T(8,128)} fusion(f32[6016,1024]{0,1:T(8,128)} %copy.13, f32[1024,1024]{1,0:T(8,128)} %reduce_sum.18, f32[6016,1024]{1,0:T(8,128)} %bitcast.37), kind=kOutput, calls=%fused_computation.1 | convolution fusion | flops 75704958976 | bytes 78118912 | tf_op jit(solution)/shard_map/dot_general | solution.py:15
  692.1 0.0 copy-done
  692.1 6.0 convolution_bitcast_fusion
  698.1 0.0 all-gather.13.cloned.1.call-update
  698.1 0.0 all-gather.9.cloned.1.call-start
  698.2 0.5 all-gather.9.cloned.1.call-update
  698.7 288.2 %all-gather.13.cloned.1.call-done = f32[8192,1024]{0,1:T(8,128)} async-done(((f32[1024,1024]{0,1:T(8,128)}), f32[8192,1024]{0,1:T(8,128)}) %all-gather.13.cloned.1.call-update) | async-done | bytes 33554448 | tf_op jit(solution)/shard_map/all_gather | solution.py:9
  986.9 34.9 %copy.16 = f32[128,8,8,1024]{3,2,1,0:T(8,128)S(1)} copy(f32[128,8,8,1024]{3,1,2,0:T(8,128)} %bitcast.33) | data formatting | bytes 67108864
  1021.8 12.6 bitcast_reduce_fusion
  1034.5 5.4 copy.14
  1039.8 166.0 %all-gather.9.cloned.1.call-done = f32[46,128,1024]{2,1,0:T(8,128)} async-done(((f32[46,128,256]{2,1,0:T(8,128)}), f32[46,128,1024]{2,1,0:T(8,128)}) %all-gather.9.cloned.1.call-update) | async-done | bytes 24117264 | tf_op jit(solution)/shard_map/all_gather | solution.py:27
  1205.8 85.5 %slice_subtract_fusion = f32[5888,1024]{0,1:T(8,128)} fusion(f32[6016,1024]{0,1:T(8,128)} %bitcast_subtract_fusion, f32[1024,1024]{0,1:T(8,128)} %bitcast_reduce_fusion, f32[5888,1024]{1,0:T(8,128)} %bitcast.38), kind=kOutput, calls=%fused_computation.2 | convolution fusion | flops 74094215168 | bytes 76546048 | tf_op jit(solution)/shard_map/dot_general | solution.py:15
  1291.2 24.1 %copy.15 = f32[5888,1024]{1,0:T(8,128)} copy(f32[5888,1024]{0,1:T(8,128)} %slice_subtract_fusion) | data formatting | bytes 48234496 | tf_op jit(solution)/shard_map/sub | solution.py:26
  1315.3 8.5 pad_maximum_fusion
Async XLA Ops:
  7.2 298.2 %all-gather.11.cloned.1.call-start = ((), (), s32[]{:S(2)}) async-start(), calls=%async_computation.2 | async-start | bytes 37748736 | tf_op jit(solution)/shard_map/all_gather | solution.py:9
  13.9 514.8 %all-gather.7.cloned.1.call-start = ((), (), s32[]{:S(2)}) async-start(), calls=%async_computation | async-start | bytes 30801920 | tf_op jit(solution)/shard_map/all_gather | solution.py:22
  14.6 972.3 %all-gather.13.cloned.1.call-start = ((), (), s32[]{:S(2)}) async-start(), calls=%async_computation.3 | async-start | bytes 37748736 | tf_op jit(solution)/shard_map/all_gather | solution.py:9
  528.7 163.4 %copy-start = (f32[2,1024,128]{2,1,0:T(8,128)S(1)}, f32[2,1024,128]{2,1,0:T(8,128)}, u32[]{:S(2)}) copy-start(f32[2,1024,128]{2,1,0:T(8,128)} %param.7) | copy-start | bytes 3145732
  698.1 507.7 %all-gather.9.cloned.1.call-start = ((), (), s32[]{:S(2)}) async-start(), calls=%async_computation.1 | async-start | bytes 30146560 | tf_op jit(solution)/shard_map/all_gather | solution.py:27
Sparse Core Ops, SparseCore 0:
  14.0 291.3 all-gather.10
  307.2 221.4 all-gather.6
  698.2 288.6 all-gather.12
  988.6 217.1 all-gather.8
